TPU v7x, 32 devices: a whole 2x2x4 slice. The times are simulated.
32 devices in a mesh: cluster: 4 (over z), sub: 8 (over y, x, core).
Axes of the slice: x: 2, y: 2, z: 4, core: 2. Of those that a mesh axis runs over, the one named last changes fastest.
Arguments:
- dual_operators: bfloat16 [64, 2048, 2048], P(('cluster', 'sub')), may hold values from -1 to 3, as said below
- local_loads: float32 [64, 2048, 128], P(('cluster', 'sub')), may hold values from -15 to 15
- modes: float32 [64, 6, 2048], P(('cluster', 'sub')), may hold values from -4 to 4
- coarse_matrix: float32 [384, 384], P(('cluster', 'sub')), may hold values from -1 to 1, as said below
- coarse_loads: float32 [384, 128], replicated, may hold values from -6144 to 6144
- slot_block: int32 [32, 32], P(('cluster', 'sub')), may hold values from 0 to 31, each once within a row
Outputs:
- multipliers: float32 [64, 2048, 128], P(('cluster', 'sub'))
- projected_residual: float32 [64, 2048, 128], P(('cluster', 'sub'))
Inputs may be any that keep to these rules, and one draw needn't show every extreme that they name: `dual_operators`: each subdomain's matrix is symmetric and positive definite. `coarse_matrix`: Symmetric.
All inputs are finite; a program needn't handle non-finite values.
Results may differ from a plain program's by a relative error of at most 0.0018.
Values sent between devices are 32-bit elements; how exact they have to be, the bound alone decides.
A program may use at most 128 MiB of HBM per device.

v0:
```python
import jax
import jax.numpy as jnp
from jax import lax
from jax.sharding import PartitionSpec as P

NMODE = 6
ITERS = 3


def from_behind(value, axis, steps):
    count = lax.axis_size(axis)
    initial, last = (max(0, -steps), min(count, count - steps))
    return lax.ppermute(value, axis, [(source, source + steps) for source in range(initial, last)])


def with_halo(shard, sides, width):
    for axis, dim in sides:
        size, length = (lax.axis_size(axis), shard.shape[dim])
        up = [(i, (i + 1) % size) for i in range(size - 1)]
        down = [(j, i) for i, j in up]
        last = lax.slice_in_dim(shard, length - width, length, axis=dim)
        initial = lax.slice_in_dim(shard, 0, width, axis=dim)
        before = lax.ppermute(last, axis, up)
        after = lax.ppermute(initial, axis, down)
        shard = jnp.concatenate([before, shard, after], axis=dim)
    return shard


def on_device(dual_operators, local_loads, modes, coarse_matrix, coarse_loads, slot_block):
    highest = lax.Precision.HIGHEST
    slot_order = slot_block[0]
    block_total = slot_order.shape[0]
    face_size = block_total // 8
    local_count, dual_order, load_count = local_loads.shape
    block_count = block_total // local_count
    block_size = dual_order // block_count
    peer_count = lax.axis_size("sub")
    cluster_total = lax.axis_size("cluster")
    own_index = lax.axis_index("sub")
    cluster_index = lax.axis_index("cluster")
    positions = jnp.arange(block_total, dtype=jnp.int32)
    inverse = jnp.sum(
        positions[:, None] * (slot_order[:, None] == positions[None, :]).astype(jnp.int32), axis=0
    )
    face_ids = positions // face_size
    shared = (
        (face_ids == 0) & (own_index > 0)
        | (face_ids == 1) & (own_index < peer_count - 1)
        | (face_ids == 2) & (cluster_index > 0)
        | (face_ids == 3) & (cluster_index < cluster_total - 1)
        | (face_ids >= 6)
    )
    slot_weights = jnp.where(shared, 0.5, 1.0).astype(jnp.float32)
    weights = jnp.repeat(slot_weights[inverse], block_size).reshape(local_count, dual_order)
    coeff_rows = local_count * NMODE

    def to_slots(values):
        return values.reshape(block_total, block_size, values.shape[-1])[slot_order]

    def from_slots(slot_values):
        return slot_values[inverse].reshape(local_count, dual_order, slot_values.shape[-1])

    def receive(slot_values):
        trailing = slot_values.shape[1:]
        outer = slot_values[: 4 * face_size].reshape((4, face_size) + trailing)
        lower_sub = from_behind(outer[1], "sub", 1)
        upper_sub = from_behind(outer[0], "sub", -1)
        lower_cluster = from_behind(outer[3], "cluster", 1)
        upper_cluster = from_behind(outer[2], "cluster", -1)
        blank_faces = jnp.zeros((2 * face_size,) + trailing, jnp.float32)
        return jnp.concatenate(
            [
                lower_sub,
                upper_sub,
                lower_cluster,
                upper_cluster,
                blank_faces,
                slot_values[7 * face_size : 8 * face_size],
                slot_values[6 * face_size : 7 * face_size],
            ],
            axis=0,
        )

    def assemble(values):
        sent = to_slots(values)
        return from_slots(sent - receive(sent))

    def apply_dual(direction):
        local_image = jnp.einsum(
            "smn,snl->sml",
            dual_operators,
            direction.astype(jnp.bfloat16),
            preferred_element_type=jnp.float32,
        )
        return assemble(local_image)

    def spread_modes(coeff):
        return jnp.einsum(
            "srm,srl->sml", modes, coeff.reshape(local_count, NMODE, load_count), precision=highest
        )

    def coarse_coefficients(values):
        coarse_terms = jnp.einsum("srm,sml->srl", modes, values, precision=highest).reshape(
            coeff_rows, load_count
        )
        return jnp.dot(
            coarse_matrix,
            lax.all_gather(coarse_terms, ("cluster", "sub"), axis=0, tiled=True),
            precision=highest,
        )

    def inner_product(left, right):
        return jnp.sum(weights[:, :, None] * left * right, axis=(0, 1))

    def residual_norm(values):
        return lax.psum(inner_product(values, values), ("cluster", "sub"))

    block_modes = (
        modes.reshape(local_count, NMODE, block_count, block_size)
        .transpose(0, 2, 1, 3)
        .reshape(block_total, NMODE, block_size)
    )
    owner_mask = (
        positions[:, None] // block_count == jnp.arange(local_count, dtype=jnp.int32)[None, :]
    ).astype(jnp.float32)
    spread_rows = (owner_mask[:, :, None, None] * block_modes[:, None]).reshape(
        block_total, coeff_rows, block_size
    )[slot_order]
    fetched = receive(spread_rows)

    def correct(coeff):
        own_part = to_slots(spread_modes(coeff))
        beside_all = with_halo(coeff[None, None], (("cluster", 0), ("sub", 1)), 1)
        sources = jnp.stack(
            [beside_all[1, 0], beside_all[1, 2], beside_all[0, 1], beside_all[2, 1]], axis=0
        )
        outer_part = jnp.einsum(
            "fkrm,frl->fkml",
            fetched[: 4 * face_size].reshape(4, face_size, coeff_rows, block_size),
            sources,
            precision=highest,
        ).reshape(4 * face_size, block_size, load_count)
        inside_part = jnp.einsum("krm,rl->kml", fetched[6 * face_size :], coeff, precision=highest)
        blank_part = jnp.zeros((2 * face_size, block_size, load_count), jnp.float32)
        partner_part = jnp.concatenate([outer_part, blank_part, inside_part], axis=0)
        return from_slots(own_part - partner_part)

    initial_coeff = jnp.dot(coarse_matrix, coarse_loads, precision=highest)
    dual_rhs = assemble(local_loads)
    multipliers = correct(initial_coeff)
    residual = dual_rhs - apply_dual(multipliers)
    projected = residual - correct(coarse_coefficients(residual))
    gamma_now = residual_norm(projected)
    direction = projected
    for iteration in range(ITERS):
        image_dir = apply_dual(direction)
        curvature_sum = lax.psum(inner_product(direction, image_dir), ("cluster", "sub"))
        step_size = gamma_now / curvature_sum
        multipliers = multipliers + step_size * direction
        residual = residual - step_size * image_dir
        projected = residual - correct(coarse_coefficients(residual))
        if iteration + 1 < ITERS:
            gamma_next = residual_norm(projected)
            direction = projected + gamma_next / gamma_now * direction
            gamma_now = gamma_next
    return (multipliers, projected)


def solution(mesh):
    return jax.shard_map(
        on_device,
        mesh=mesh,
        in_specs=(
            P(("cluster", "sub"), None, None),
            P(("cluster", "sub"), None, None),
            P(("cluster", "sub"), None, None),
            P(("cluster", "sub"), None),
            P(),
            P(("cluster", "sub"), None),
        ),
        out_specs=(P(("cluster", "sub"), None, None), P(("cluster", "sub"), None, None)),
        check_vma=False,
    )
```

profile of v0, /device:TPU:0, one launch (start us, length us, event | category | flops | bytes accessed | tf_op | source)
XLA Modules:
  0.0 781.1 jit_solution(5334320793376755527)
XLA Ops:
  3.3 5.6 collective-permute-start.4
  18.2 4.5 collective-permute-start.2
  32.5 4.4 collective-permute-start.6
  37.7 3.7 collective-permute-start
  42.8 4.2 collective-permute-start.10
  55.3 13.1 %convolution_bitcast_fusion.7 = f32[2,2048,128]{1,2,0:T(8,128)} fusion(bf16[2,2048,128]{2,1,0:T(8,128)(2,1)} %bitcast_convert_fusion, bf16[2,2048,2048]{2,1,0:T(8,128)(2,1)} %param.6), kind=kOutput, calls=%fused_computation.38 | convolution fusion | flops 2147483648 | bytes 19922944 | tf_op jit(solution)/shard_map/smn,snl->sml/dot_general | solution.py:89
  71.4 3.6 gather_fusion.6
  77.3 4.6 collective-permute-start.12
  84.2 5.0 collective-permute-start.14
  95.6 3.6 gather_fusion.5
  103.1 3.6 gather_fusion.7
  110.5 45.0 %all-gather = f32[32,12,128]{2,1,0:T(8,128)S(1)} all-gather(f32[1,12,128]{2,1,0:T(8,128)S(1)} %reshape.505), channel_id=1, replica_groups=mesh['cluster'=4,'sub'=8] {'cluster','sub'}, dimensions={0}, use_global_device_ids=true | all-gather | bytes 202752 | tf_op jit(solution)/shard_map/all_gather | solution.py:108
  157.1 4.5 collective-permute-start.16
  161.6 3.2 convolution_bitcast_fusion.6
  170.0 3.6 gather_fusion.8
  173.6 3.0 collective-permute-start.18
  179.3 3.2 fusion.7
  182.5 3.6 gather_fusion.9
  186.1 3.1 bitcast_subtract_fusion.3
  189.2 12.1 %convolution_bitcast_fusion.5 = f32[2,2048,128]{1,2,0:T(8,128)S(1)} fusion(bf16[2,2048,2048]{2,1,0:T(8,128)(2,1)} %param.6, f32[2,2048,128]{2,1,0:T(8,128)} %bitcast_subtract_fusion.3), kind=kOutput, calls=%fused_computation.36 | convolution fusion | flops 2148007936 | bytes 20971520 | tf_op jit(solution)/shard_map/smn,snl->sml/dot_general | solution.py:89
  206.5 3.0 collective-permute-start.20
  219.0 5.1 collective-permute-done.23
  225.9 3.7 gather_fusion.11
  229.7 4.2 fusion.1
  233.8 41.1 %all-reduce = (f32[128]{0:T(128)S(1)}, f32[128]{0:T(128)S(1)}) all-reduce(f32[128]{0:T(128)S(1)} %get-tuple-element.3, f32[128]{0:T(128)S(1)} %get-tuple-element.2), channel_id=1, replica_groups=mesh['cluster'=4,'sub'=8] {'cluster','sub'}, use_global_device_ids=true, to_apply=%region_2.3 | all-reduce | flops 256 | bytes 2048 | tf_op jit(solution)/shard_map/psum | solution.py:116
  279.4 41.9 %all-gather.1 = f32[32,12,128]{2,1,0:T(8,128)S(1)} all-gather(f32[1,12,128]{2,1,0:T(8,128)S(1)} %reshape.507), channel_id=1, replica_groups=mesh['cluster'=4,'sub'=8] {'cluster','sub'}, dimensions={0}, use_global_device_ids=true | all-gather | bytes 202752 | tf_op jit(solution)/shard_map/all_gather | solution.py:108
  322.9 4.7 collective-permute-start.24
  327.6 3.2 convolution_bitcast_fusion.4
  336.2 3.7 gather_fusion.12
  339.8 3.0 collective-permute-start.26
  345.5 3.3 fusion.9
  348.8 3.6 gather_fusion.13
  352.4 4.4 fusion.2
  356.8 39.3 %psum.44 = f32[128]{0:T(128)S(1)} all-reduce(f32[128]{0:T(128)S(1)} %get-tuple-element.8), channel_id=1, replica_groups=mesh['cluster'=4,'sub'=8] {'cluster','sub'}, use_global_device_ids=true, to_apply=%region_6.7 | all-reduce | flops 128 | bytes 1024 | tf_op jit(solution)/shard_map/psum | solution.py:116
  396.1 4.5 fusion.17
  400.7 13.4 %convolution_bitcast_fusion.3 = f32[2,2048,128]{1,2,0:T(8,128)} fusion(bf16[2,2048,2048]{2,1,0:T(8,128)(2,1)} %param.6, f32[2,2048,128]{2,1,0:T(8,128)} %fusion.17), kind=kOutput, calls=%fused_computation.34 | convolution fusion | flops 2148007936 | bytes 20971520 | tf_op jit(solution)/shard_map/smn,snl->sml/dot_general | solution.py:89
  417.0 3.6 gather_fusion.14
  424.6 3.6 collective-permute-start.30
  432.2 4.7 collective-permute-done.31
  438.5 3.6 gather_fusion.15
  442.2 3.6 multiply_reduce_fusion.1
  445.8 43.6 %psum.45 = f32[128]{0:T(128)S(1)} all-reduce(f32[128]{0:T(128)S(1)} %multiply_reduce_fusion.1), channel_id=1, replica_groups=mesh['cluster'=4,'sub'=8] {'cluster','sub'}, use_global_device_ids=true, to_apply=%region_8.9 | all-reduce | flops 128 | bytes 1024 | tf_op jit(solution)/shard_map/psum | solution.py:157
  494.4 41.3 %all-gather.2 = f32[32,12,128]{2,1,0:T(8,128)S(1)} all-gather(f32[1,12,128]{2,1,0:T(8,128)S(1)} %reshape.509), channel_id=1, replica_groups=mesh['cluster'=4,'sub'=8] {'cluster','sub'}, dimensions={0}, use_global_device_ids=true | all-gather | bytes 202752 | tf_op jit(solution)/shard_map/all_gather | solution.py:108
  537.3 4.5 collective-permute-start.32
  541.9 3.2 convolution_bitcast_fusion.2
  550.3 3.6 gather_fusion.16
  553.8 3.0 collective-permute-start.34
  559.5 3.2 fusion.11
  562.7 3.6 gather_fusion.17
  566.3 5.2 fusion.3
  571.5 39.7 %psum.46 = f32[128]{0:T(128)S(1)} all-reduce(f32[128]{0:T(128)S(1)} %get-tuple-element.6), channel_id=1, replica_groups=mesh['cluster'=4,'sub'=8] {'cluster','sub'}, use_global_device_ids=true, to_apply=%region_10.11 | all-reduce | flops 128 | bytes 1024 | tf_op jit(solution)/shard_map/psum | solution.py:116
  611.3 3.2 fusion.15
  614.4 13.5 %convolution_bitcast_fusion.1 = f32[2,2048,128]{1,2,0:T(8,128)} fusion(bf16[2,2048,2048]{2,1,0:T(8,128)(2,1)} %param.6, f32[2,2048,128]{2,1,0:T(8,128)S(1)} %fusion.15), kind=kOutput, calls=%fused_computation.32 | convolution fusion | flops 2148007936 | bytes 20971520 | tf_op jit(solution)/shard_map/smn,snl->sml/dot_general | solution.py:89
  635.8 3.6 collective-permute-start.38
  643.4 4.7 collective-permute-done.39
  649.8 3.6 gather_fusion.19
  653.3 4.6 multiply_reduce_fusion
  657.9 43.6 %psum.47 = f32[128]{0:T(128)S(1)} all-reduce(f32[128]{0:T(128)S(1)} %multiply_reduce_fusion), channel_id=1, replica_groups=mesh['cluster'=4,'sub'=8] {'cluster','sub'}, use_global_device_ids=true, to_apply=%region_12.13 | all-reduce | flops 128 | bytes 1024 | tf_op jit(solution)/shard_map/psum | solution.py:157
  701.5 6.0 fusion.14
  710.1 41.3 %all-gather.3 = f32[32,12,128]{2,1,0:T(8,128)S(1)} all-gather(f32[1,12,128]{2,1,0:T(8,128)S(1)} %reshape.511), channel_id=1, replica_groups=mesh['cluster'=4,'sub'=8] {'cluster','sub'}, dimensions={0}, use_global_device_ids=true | all-gather | bytes 202752 | tf_op jit(solution)/shard_map/all_gather | solution.py:108
  753.0 4.7 collective-permute-start.40
  766.0 3.0 collective-permute-start.42
  773.4 3.6 gather_fusion.21
  777.0 3.9 bitcast_subtract_fusion
  (246 shorter events, 150.2 us)
Async XLA Ops:
  0.6 8.9 %copy-start = (f32[2,2048,128]{2,1,0:T(8,128)S(1)}, f32[2,2048,128]{2,1,0:T(8,128)}, u32[]{:S(2)}) copy-start(f32[2,2048,128]{2,1,0:T(8,128)} %param.7) | copy-start | bytes 6291460
  2.0 23.8 %collective-permute-start.5 = (f32[1,1,12,128]{3,2,1,0:T(8,128)S(1)}, f32[1,1,12,128]{3,2,1,0:T(8,128)S(1)}, u32[]{:S(2)}, u32[]{:S(2)}) collective-permute-start(f32[1,1,12,128]{3,2,1,0:T(8,128)S(1)} %bitcast.249), channel_id=1, source_target_pairs={{8,0},{16,8},{24,16},{9,1},{17,9},{25,17},{10,2},{18,10},{26,18},{... | collective-permute-start | bytes 18440 | tf_op jit(solution)/shard_map/ppermute | solution.py:24
  3.3 23.8 %collective-permute-start.4 = (f32[1,1,12,128]{3,2,1,0:T(8,128)S(1)}, f32[1,1,12,128]{3,2,1,0:T(8,128)S(1)}, u32[]{:S(2)}, u32[]{:S(2)}) collective-permute-start(f32[1,1,12,128]{3,2,1,0:T(8,128)S(1)} %bitcast.250), channel_id=1, source_target_pairs={{0,8},{8,16},{16,24},{1,9},{9,17},{17,25},{2,10},{10,18},{18,26},{... | collective-permute-start | bytes 18440 | tf_op jit(solution)/shard_map/ppermute | solution.py:23
  11.5 4.4 copy-start.10
  11.5 11.3 %copy-start.17 = (s32[1,32]{1,0:T(1,128)S(1)}, s32[1,32]{1,0:T(1,128)}, u32[]{:S(2)}) copy-start(s32[1,32]{1,0:T(1,128)} %param.11) | copy-start | bytes 388
  13.7 68.2 %collective-permute-start.8 = (f32[4,128,128]{2,1,0:T(8,128)}, f32[4,128,128]{2,1,0:T(8,128)}, u32[]{:S(2)}, u32[]{:S(2)}) collective-permute-start(f32[4,128,128]{2,1,0:T(8,128)} %get-tuple-element.30), channel_id=1, source_target_pairs={{0,1},{1,2},{2,3},{3,4},{4,5},{5,6},{6,7},{8,9},{9,10},{10,11},{11... | collective-permute-start | bytes 786440 | tf_op jit(solution)/shard_map/ppermute | solution.py:13
  16.9 24.6 %collective-permute-start.3 = (f32[4,12,128]{2,1,0:T(8,128)S(1)}, f32[4,12,128]{2,1,0:T(8,128)S(1)}, u32[]{:S(2)}, u32[]{:S(2)}) collective-permute-start(f32[4,12,128]{2,1,0:T(8,128)S(1)} %get-tuple-element.33), channel_id=1, source_target_pairs={{8,0},{16,8},{24,16},{9,1},{17,9},{25,17},{10,2},{18,10},{26,18},{... | collective-permute-start | bytes 73736 | tf_op jit(solution)/shard_map/ppermute | solution.py:13
  18.2 24.6 %collective-permute-start.2 = (f32[4,12,128]{2,1,0:T(8,128)S(1)}, f32[4,12,128]{2,1,0:T(8,128)S(1)}, u32[]{:S(2)}, u32[]{:S(2)}) collective-permute-start(f32[4,12,128]{2,1,0:T(8,128)S(1)} %get-tuple-element.34), channel_id=1, source_target_pairs={{0,8},{8,16},{16,24},{1,9},{9,17},{17,25},{2,10},{10,18},{18,26},{... | collective-permute-start | bytes 73736 | tf_op jit(solution)/shard_map/ppermute | solution.py:13
  25.8 21.2 %collective-permute-start.1 = (f32[4,12,128]{2,1,0:T(8,128)S(1)}, f32[4,12,128]{2,1,0:T(8,128)S(1)}, u32[]{:S(2)}, u32[]{:S(2)}) collective-permute-start(f32[4,12,128]{2,1,0:T(8,128)S(1)} %get-tuple-element.35), channel_id=1, source_target_pairs={{1,0},{2,1},{3,2},{4,3},{5,4},{6,5},{7,6},{9,8},{10,9},{11,10},{12... | collective-permute-start | bytes 73736 | tf_op jit(solution)/shard_map/ppermute | solution.py:13
  27.1 5.4 collective-permute-start.7
  32.5 5.2 collective-permute-start.6
  37.7 10.5 %collective-permute-start = (f32[4,12,128]{2,1,0:T(8,128)S(1)}, f32[4,12,128]{2,1,0:T(8,128)S(1)}, u32[]{:S(2)}, u32[]{:S(2)}) collective-permute-start(f32[4,12,128]{2,1,0:T(8,128)S(1)} %get-tuple-element.31), channel_id=1, source_target_pairs={{0,1},{1,2},{2,3},{3,4},{4,5},{5,6},{6,7},{8,9},{9,10},{10,11},{11... | collective-permute-start | bytes 73736 | tf_op jit(solution)/shard_map/ppermute | solution.py:13
  41.5 42.7 %collective-permute-start.9 = (f32[4,128,128]{2,1,0:T(8,128)}, f32[4,128,128]{2,1,0:T(8,128)}, u32[]{:S(2)}, u32[]{:S(2)}) collective-permute-start(f32[4,128,128]{2,1,0:T(8,128)} %get-tuple-element.29), channel_id=1, source_target_pairs={{1,0},{2,1},{3,2},{4,3},{5,4},{6,5},{7,6},{9,8},{10,9},{11,10},{12... | collective-permute-start | bytes 786440 | tf_op jit(solution)/shard_map/ppermute | solution.py:13
  42.8 47.3 %collective-permute-start.10 = (f32[4,128,128]{2,1,0:T(8,128)}, f32[4,128,128]{2,1,0:T(8,128)}, u32[]{:S(2)}, u32[]{:S(2)}) collective-permute-start(f32[4,128,128]{2,1,0:T(8,128)} %get-tuple-element.28), channel_id=1, source_target_pairs={{0,8},{8,16},{16,24},{1,9},{9,17},{17,25},{2,10},{10,18},{18,26},{... | collective-permute-start | bytes 786440 | tf_op jit(solution)/shard_map/ppermute | solution.py:13
  47.0 45.9 %collective-permute-start.11 = (f32[4,128,128]{2,1,0:T(8,128)}, f32[4,128,128]{2,1,0:T(8,128)}, u32[]{:S(2)}, u32[]{:S(2)}) collective-permute-start(f32[4,128,128]{2,1,0:T(8,128)} %get-tuple-element.27), channel_id=1, source_target_pairs={{8,0},{16,8},{24,16},{9,1},{17,9},{25,17},{10,2},{18,10},{26,18},{... | collective-permute-start | bytes 786440 | tf_op jit(solution)/shard_map/ppermute | solution.py:13
  54.1 14.3 %copy-start.9 = (f32[32,128,128]{2,1,0:T(8,128)}, f32[32,128,128]{2,1,0:T(8,128)S(1)}, u32[]{:S(2)}) copy-start(f32[32,128,128]{2,1,0:T(8,128)S(1)} %gather_fusion.2) | copy-start | bytes 6291460
  75.0 18.9 %copy-start.11 = (f32[32,128,128]{2,1,0:T(8,128)S(1)}, f32[32,128,128]{2,1,0:T(8,128)}, u32[]{:S(2)}) copy-start(f32[32,128,128]{2,1,0:T(8,128)} %gather_fusion.4) | copy-start | bytes 6291460
  77.3 21.9 %collective-permute-start.12 = (f32[4,128,128]{2,1,0:T(8,128)}, f32[4,128,128]{2,1,0:T(8,128)S(1)}, u32[]{:S(2)}, u32[]{:S(2)}) collective-permute-start(f32[4,128,128]{2,1,0:T(8,128)} %get-tuple-element.26), channel_id=1, source_target_pairs={{0,1},{1,2},{2,3},{3,4},{4,5},{5,6},{6,7},{8,9},{9,10},{10,11},{11... | collective-permute-start | bytes 786440 | tf_op jit(solution)/shard_map/ppermute | solution.py:13
  81.9 17.3 %collective-permute-start.13 = (f32[4,128,128]{2,1,0:T(8,128)}, f32[4,128,128]{2,1,0:T(8,128)S(1)}, u32[]{:S(2)}, u32[]{:S(2)}) collective-permute-start(f32[4,128,128]{2,1,0:T(8,128)} %get-tuple-element.25), channel_id=1, source_target_pairs={{1,0},{2,1},{3,2},{4,3},{5,4},{6,5},{7,6},{9,8},{10,9},{11,10},{12... | collective-permute-start | bytes 786440 | tf_op jit(solution)/shard_map/ppermute | solution.py:13
  84.2 15.1 %collective-permute-start.14 = (f32[4,128,128]{2,1,0:T(8,128)}, f32[4,128,128]{2,1,0:T(8,128)}, u32[]{:S(2)}, u32[]{:S(2)}) collective-permute-start(f32[4,128,128]{2,1,0:T(8,128)} %get-tuple-element.24), channel_id=1, source_target_pairs={{0,8},{8,16},{16,24},{1,9},{9,17},{17,25},{2,10},{10,18},{18,26},{... | collective-permute-start | bytes 786440 | tf_op jit(solution)/shard_map/ppermute | solution.py:13
  90.1 10.2 %collective-permute-start.15 = (f32[4,128,128]{2,1,0:T(8,128)}, f32[4,128,128]{2,1,0:T(8,128)}, u32[]{:S(2)}, u32[]{:S(2)}) collective-permute-start(f32[4,128,128]{2,1,0:T(8,128)} %get-tuple-element.23), channel_id=1, source_target_pairs={{8,0},{16,8},{24,16},{9,1},{17,9},{25,17},{10,2},{18,10},{26,18},{... | collective-permute-start | bytes 786440 | tf_op jit(solution)/shard_map/ppermute | solution.py:13
  99.2 2.2 copy-start.12
  109.2 76.9 %copy-start.2 = (f32[32,128,128]{2,1,0:T(8,128)}, f32[32,128,128]{2,1,0:T(8,128)S(1)}, u32[]{:S(2)}) copy-start(f32[32,128,128]{2,1,0:T(8,128)S(1)} %sub.113) | copy-start | bytes 6291460
  109.2 46.3 %copy-start.16 = (f32[12,384]{1,0:T(8,128)S(1)}, f32[12,384]{1,0:T(8,128)}, u32[]{:S(2)}) copy-start(f32[12,384]{1,0:T(8,128)} %param.9) | copy-start | bytes 55300
  155.8 9.0 %collective-permute-start.17 = (f32[1,1,12,128]{3,2,1,0:T(8,128)S(1)}, f32[1,1,12,128]{3,2,1,0:T(8,128)S(1)}, u32[]{:S(2)}, u32[]{:S(2)}) collective-permute-start(f32[1,1,12,128]{3,2,1,0:T(8,128)S(1)} %bitcast.256), channel_id=1, source_target_pairs={{8,0},{16,8},{24,16},{9,1},{17,9},{25,17},{10,2},{18,10},{26,18},{... | collective-permute-start | bytes 18440 | tf_op jit(solution)/shard_map/ppermute | solution.py:24
  157.1 7.7 collective-permute-start.16
  164.8 11.8 %collective-permute-start.19 = (f32[3,1,12,128]{3,2,1,0:T(8,128)S(1)}, f32[3,1,12,128]{3,2,1,0:T(8,128)S(1)}, u32[]{:S(2)}, u32[]{:S(2)}) collective-permute-start(f32[3,1,12,128]{3,2,1,0:T(8,128)S(1)} %pad_maximum_fusion.8), channel_id=1, source_target_pairs={{1,0},{2,1},{3,2},{4,3},{5,4},{6,5},{7,6},{9,8},{10,9},{11,10},{12... | collective-permute-start | bytes 55304 | tf_op jit(solution)/shard_map/ppermute | solution.py:24
  173.6 3.9 collective-permute-start.18
  205.4 5.4 copy-start.13
  206.5 9.4 %collective-permute-start.20 = (f32[4,128,128]{2,1,0:T(8,128)}, f32[4,128,128]{2,1,0:T(8,128)S(1)}, u32[]{:S(2)}, u32[]{:S(2)}) collective-permute-start(f32[4,128,128]{2,1,0:T(8,128)} %get-tuple-element.22), channel_id=1, source_target_pairs={{0,1},{1,2},{2,3},{3,4},{4,5},{5,6},{6,7},{8,9},{9,10},{10,11},{11... | collective-permute-start | bytes 786440 | tf_op jit(solution)/shard_map/ppermute | solution.py:13
  209.5 6.4 collective-permute-start.21
  210.8 7.2 collective-permute-start.22
  214.4 9.7 %copy-start.14 = (f32[32,128,128]{2,1,0:T(8,128)S(1)}, f32[32,128,128]{2,1,0:T(8,128)}, u32[]{:S(2)}) copy-start(f32[32,128,128]{2,1,0:T(8,128)} %copy-done.13) | copy-start | bytes 6291460
  214.4 9.7 %collective-permute-start.23 = (f32[4,128,128]{2,1,0:T(8,128)}, f32[4,128,128]{2,1,0:T(8,128)S(1)}, u32[]{:S(2)}, u32[]{:S(2)}) collective-permute-start(f32[4,128,128]{2,1,0:T(8,128)} %get-tuple-element.19), channel_id=1, source_target_pairs={{8,0},{16,8},{24,16},{9,1},{17,9},{25,17},{10,2},{18,10},{26,18},{... | collective-permute-start | bytes 786440 | tf_op jit(solution)/shard_map/ppermute | solution.py:13
  225.9 3.8 copy-start.3
  275.0 1.8 copy-start.18
  276.8 1.4 copy-start.6
  321.6 9.3 %collective-permute-start.25 = (f32[1,1,12,128]{3,2,1,0:T(8,128)S(1)}, f32[1,1,12,128]{3,2,1,0:T(8,128)S(1)}, u32[]{:S(2)}, u32[]{:S(2)}) collective-permute-start(f32[1,1,12,128]{3,2,1,0:T(8,128)S(1)} %bitcast.260), channel_id=1, source_target_pairs={{8,0},{16,8},{24,16},{9,1},{17,9},{25,17},{10,2},{18,10},{26,18},{... | collective-permute-start | bytes 18440 | tf_op jit(solution)/shard_map/ppermute | solution.py:24
  322.9 8.0 %collective-permute-start.24 = (f32[1,1,12,128]{3,2,1,0:T(8,128)S(1)}, f32[1,1,12,128]{3,2,1,0:T(8,128)S(1)}, u32[]{:S(2)}, u32[]{:S(2)}) collective-permute-start(f32[1,1,12,128]{3,2,1,0:T(8,128)S(1)} %bitcast.261), channel_id=1, source_target_pairs={{0,8},{8,16},{16,24},{1,9},{9,17},{17,25},{2,10},{10,18},{18,26},{... | collective-permute-start | bytes 18440 | tf_op jit(solution)/shard_map/ppermute | solution.py:23
  330.9 12.0 %collective-permute-start.27 = (f32[3,1,12,128]{3,2,1,0:T(8,128)S(1)}, f32[3,1,12,128]{3,2,1,0:T(8,128)S(1)}, u32[]{:S(2)}, u32[]{:S(2)}) collective-permute-start(f32[3,1,12,128]{3,2,1,0:T(8,128)S(1)} %pad_maximum_fusion.9), channel_id=1, source_target_pairs={{1,0},{2,1},{3,2},{4,3},{5,4},{6,5},{7,6},{9,8},{10,9},{11,10},{12... | collective-permute-start | bytes 55304 | tf_op jit(solution)/shard_map/ppermute | solution.py:24
  339.8 3.9 collective-permute-start.26
  352.4 43.7 %copy-start.19 = (f32[128]{0:T(128)S(1)}, f32[128]{0:T(128)}, u32[]{:S(2)}) copy-start(f32[128]{0:T(128)} %copy-done.18) | copy-start | bytes 1540
  420.6 16.4 %copy-start.15 = (f32[32,128,128]{2,1,0:T(8,128)S(1)}, f32[32,128,128]{2,1,0:T(8,128)}, u32[]{:S(2)}) copy-start(f32[32,128,128]{2,1,0:T(8,128)} %gather_fusion.14) | copy-start | bytes 6291460
  422.0 7.7 collective-permute-start.28
  423.3 6.5 collective-permute-start.29
  424.6 7.5 collective-permute-start.30
  428.2 8.6 %collective-permute-start.31 = (f32[4,128,128]{2,1,0:T(8,128)S(1)}, f32[4,128,128]{2,1,0:T(8,128)S(1)}, u32[]{:S(2)}, u32[]{:S(2)}) collective-permute-start(f32[4,128,128]{2,1,0:T(8,128)S(1)} %get-tuple-element.15), channel_id=1, source_target_pairs={{8,0},{16,8},{24,16},{9,1},{17,9},{25,17},{10,2},{18,10},{26,18},{... | collective-permute-start | bytes 786440 | tf_op jit(solution)/shard_map/ppermute | solution.py:13
  491.8 1.4 copy-start.5
  536.0 9.0 %collective-permute-start.33 = (f32[1,1,12,128]{3,2,1,0:T(8,128)S(1)}, f32[1,1,12,128]{3,2,1,0:T(8,128)S(1)}, u32[]{:S(2)}, u32[]{:S(2)}) collective-permute-start(f32[1,1,12,128]{3,2,1,0:T(8,128)S(1)} %bitcast.264), channel_id=1, source_target_pairs={{8,0},{16,8},{24,16},{9,1},{17,9},{25,17},{10,2},{18,10},{26,18},{... | collective-permute-start | bytes 18440 | tf_op jit(solution)/shard_map/ppermute | solution.py:24
  537.3 7.7 collective-permute-start.32
  545.1 11.8 %collective-permute-start.35 = (f32[3,1,12,128]{3,2,1,0:T(8,128)S(1)}, f32[3,1,12,128]{3,2,1,0:T(8,128)}, u32[]{:S(2)}, u32[]{:S(2)}) collective-permute-start(f32[3,1,12,128]{3,2,1,0:T(8,128)S(1)} %pad_maximum_fusion.10), channel_id=1, source_target_pairs={{1,0},{2,1},{3,2},{4,3},{5,4},{6,5},{7,6},{9,8},{10,9},{11,10},{12... | collective-permute-start | bytes 55304 | tf_op jit(solution)/shard_map/ppermute | solution.py:24
  553.8 3.9 collective-permute-start.34
  614.4 13.5 %copy-start.7 = (f32[2,2048,128]{2,1,0:T(8,128)}, f32[2,2048,128]{2,1,0:T(8,128)S(1)}, u32[]{:S(2)}) copy-start(f32[2,2048,128]{2,1,0:T(8,128)S(1)} %fusion.15) | copy-start | bytes 6291460
  633.2 7.5 collective-permute-start.36
  634.5 6.2 collective-permute-start.37
  635.8 7.5 collective-permute-start.38
  639.4 8.6 %collective-permute-start.39 = (f32[4,128,128]{2,1,0:T(8,128)S(1)}, f32[4,128,128]{2,1,0:T(8,128)S(1)}, u32[]{:S(2)}, u32[]{:S(2)}) collective-permute-start(f32[4,128,128]{2,1,0:T(8,128)S(1)} %get-tuple-element.11), channel_id=1, source_target_pairs={{8,0},{16,8},{24,16},{9,1},{17,9},{25,17},{10,2},{18,10},{26,18},{... | collective-permute-start | bytes 786440 | tf_op jit(solution)/shard_map/ppermute | solution.py:13
  653.3 48.2 %copy-start.4 = (f32[2,2048,128]{2,1,0:T(8,128)S(1)}, f32[2,2048,128]{2,1,0:T(8,128)}, u32[]{:S(2)}) copy-start(f32[2,2048,128]{2,1,0:T(8,128)} %bitcast_subtract_fusion.3) | copy-start | bytes 6291460
  707.5 1.3 copy-start.8
  751.7 7.9 %collective-permute-start.41 = (f32[1,1,12,128]{3,2,1,0:T(8,128)S(1)}, f32[1,1,12,128]{3,2,1,0:T(8,128)S(1)}, u32[]{:S(2)}, u32[]{:S(2)}) collective-permute-start(f32[1,1,12,128]{3,2,1,0:T(8,128)S(1)} %bitcast.252), channel_id=1, source_target_pairs={{8,0},{16,8},{24,16},{9,1},{17,9},{25,17},{10,2},{18,10},{26,18},{... | collective-permute-start | bytes 18440 | tf_op jit(solution)/shard_map/ppermute | solution.py:24
  753.0 6.6 collective-permute-start.40
  759.6 9.5 %collective-permute-start.43 = (f32[3,1,12,128]{3,2,1,0:T(8,128)S(1)}, f32[3,1,12,128]{3,2,1,0:T(8,128)S(1)}, u32[]{:S(2)}, u32[]{:S(2)}) collective-permute-start(f32[3,1,12,128]{3,2,1,0:T(8,128)S(1)} %pad_maximum_fusion.11), channel_id=1, source_target_pairs={{1,0},{2,1},{3,2},{4,3},{5,4},{6,5},{7,6},{9,8},{10,9},{11,10},{12... | collective-permute-start | bytes 55304 | tf_op jit(solution)/shard_map/ppermute | solution.py:24
  766.0 3.9 collective-permute-start.42
  777.0 3.9 copy-start.1
where the time goes:
time: 793 us; the launch traced here: 781 us
  blocking collectives  377 us (48%)
  starting transfers between devices  110 us (14%)
  local copies, waits for them, and re-layouts  108 us (14%)
  matrix products  86.6 us (11%)
  other arithmetic  72.7 us (9%)
  waiting for transfers between devices  24.9 us (3%)
    all_gather x4, blocking collectives, coarse_coefficients(): lax.all_gather(coarse_terms, ('cluster', 'sub'), axis=0, tiled=True)  170 us
    psum x3, blocking collectives, residual_norm(): return lax.psum(inner_product(values, values), ('cluster', 'sub'))  120 us
    psum x2, blocking collectives, on_device(): lax.psum(inner_product(direction, image_dir), ('cluster', 'sub'))  87.2 us
    ppermute x24, starting transfers between devices, from_behind(): lax.ppermute(value, axis, [(source, source + steps) for source in range(i...  56.2 us
    dot_general x4, matrix products, apply_dual(): jnp.einsum('smn,snl->sml', dual_operators, direction.astype(jnp.bfloat16)...  52 us
    ppermute x10, starting transfers between devices, with_halo(): before = lax.ppermute(last, axis, up)  40.6 us
    gather x10, local copies, waits for them, and re-layouts, from_slots(): slot_values[inverse].reshape(local_count, dual_order, slot_values.shape[-1])  34.8 us
    gather x10, local copies, waits for them, and re-layouts, to_slots(): return values.reshape(block_total, block_size, values.shape[-1])[slot_order]  29.1 us
  transfers between devices with their start and end apart: 44, of which 11 were waited for; matrix products, arithmetic and copies ran while one was open for 12% of the time, Pallas kernels for 0%

commit v1 on v0

v1 whole, which is shorter than its diff:
```python
import functools

import jax
import jax.numpy as jnp
from jax import lax
from jax.experimental import pallas as pl
from jax.experimental.pallas import tpu as pltpu
from jax.sharding import PartitionSpec as P

ITERS = 3
PAD = 8
LANES = 128
MESH = pl.DeviceIdType.MESH
F32, BF16 = jnp.float32, jnp.bfloat16


def split(x):
    high = x.astype(BF16)
    return high, (x - high.astype(F32)).astype(BF16)


def rows8(x):
    return jnp.sum(x.reshape(-1, 8, x.shape[-1]), axis=0)


def kernel(
    nc, ns, parts, face,
    slot_ref, inv_ref, ops_hbm, loads_hbm, modes_ref, cmat_ref, cload_ref,
    mult_out, proj_out,
    ops, ybuf, img, res, proj, dire, mult, emat, vb, halo, mslot, mfetch, mhl, call, hall, gz, gs,
    ops_sem, loads_sem, halo_send, halo_recv, m_send, m_recv, c_send, c_recv,
    zsend, zrecv, ssend, srecv, gzrecv, gsrecv,
):
    c, i = lax.axis_index("cluster"), lax.axis_index("sub")
    nblk = 8 * face
    per = nblk // parts
    blk = ybuf.shape[1]
    frows = face * blk
    unit = parts * PAD

    ops_copy = pltpu.make_async_copy(ops_hbm, ops, ops_sem)
    ops_copy.start()
    loads_copy = pltpu.make_async_copy(loads_hbm, proj, loads_sem)
    loads_copy.start()

    barrier = pltpu.get_barrier_semaphore()
    for k in range(1, nc):
        pl.semaphore_signal(barrier, inc=1, device_id=(lax.rem(c + k, nc), i), device_id_type=MESH)
    for k in range(1, ns):
        pl.semaphore_signal(barrier, inc=1, device_id=(c, lax.rem(i + k, ns)), device_id_type=MESH)

    for j in range(nblk):
        b = slot_ref[j]
        piece = modes_ref[b]
        block = jnp.broadcast_to(b, piece.shape)
        for own in range(parts):
            mine = (block >= own * per) & (block < (own + 1) * per)
            mslot[j, own * PAD:(own + 1) * PAD, :] = jnp.where(mine, piece, 0.0)
    call[0] = cmat_ref[...]

    def partner(f):
        axis, sign = f // 2, 2 * (f % 2) - 1
        tc, ti = c + axis * sign, i + (1 - axis) * sign
        there = (tc >= 0) & (tc < nc) & (ti >= 0) & (ti < ns)
        return there, (tc, ti), axis * 2 + 1 - f % 2

    def halo_copy(f, landing):
        _, device, _ = partner(f)
        return pltpu.make_async_remote_copy(
            src_ref=ybuf.at[pl.ds(f * face, face)], dst_ref=halo.at[landing],
            send_sem=halo_send.at[f], recv_sem=halo_recv.at[landing],
            device_id=device, device_id_type=MESH)

    def mode_copy(f, landing):
        _, device, _ = partner(f)
        return pltpu.make_async_remote_copy(
            src_ref=mslot.at[pl.ds(f * face, face)], dst_ref=mfetch.at[landing],
            send_sem=m_send.at[f], recv_sem=m_recv.at[landing],
            device_id=device, device_id_type=MESH)

    def coarse_copy(f, landing):
        _, device, _ = partner(f)
        return pltpu.make_async_remote_copy(
            src_ref=call.at[0], dst_ref=call.at[landing + 1],
            send_sem=c_send.at[f], recv_sem=c_recv.at[landing],
            device_id=device, device_id_type=MESH)

    pl.semaphore_wait(barrier, nc + ns - 2)
    for f in range(4):
        there, _, landing = partner(f)

        @pl.when(there)
        def _():
            mode_copy(f, landing).start()
            coarse_copy(f, landing).start()

        @pl.when(jnp.logical_not(there))
        def _():
            halo[f] = jnp.zeros(halo.shape[1:], F32)
            mfetch[f] = jnp.zeros(mfetch.shape[1:], F32)
            call[f + 1] = jnp.zeros(call.shape[1:], F32)

    for g in range(8):
        for k in range(face):
            high, low = split(mslot[g * face + k])
            mhl[g, 0:unit, k * blk:(k + 1) * blk] = high
            mhl[g, unit:2 * unit, k * blk:(k + 1) * blk] = low

    for f in range(4):
        there, _, _ = partner(f)

        @pl.when(there)
        def _():
            mode_copy(f, f).wait_recv()
            coarse_copy(f, f).wait_recv()
            mode_copy(f, f).wait_send()
            coarse_copy(f, f).wait_send()

    for g in range(8):
        for k in range(face):
            j = g * face + k
            own = mslot[j]
            if g == 6:
                own = own - mslot[j + face]
            if g == 7:
                own = own - mslot[j - face]
            pieces = [own]
            if g < 4:
                if g > 0:
                    pieces.append(jnp.zeros((g * unit, blk), F32))
                pieces.append(-mfetch[g, k])
            used = sum(x.shape[0] for x in pieces)
            pieces.append(jnp.zeros((LANES - used, blk), F32))
            high, low = split(jnp.concatenate(pieces, axis=0).T)
            emat[g, k * blk:(k + 1) * blk, 0:LANES] = high
            emat[g, k * blk:(k + 1) * blk, LANES:] = low

    cfull = call[...].reshape(5 * unit, call.shape[-1])

    def coarse(terms):
        return jnp.dot(cfull, terms, precision=lax.Precision.HIGHEST, preferred_element_type=F32)

    def spread_side(coeff):
        high, low = split(jnp.concatenate(
            [coeff, jnp.zeros((LANES - coeff.shape[0], coeff.shape[1]), F32)], axis=0))
        top = jnp.concatenate([high, low], axis=1)
        bottom = jnp.concatenate([high, jnp.zeros_like(low)], axis=1)
        return jnp.concatenate([top, bottom], axis=0)

    def correct(g, side):
        both = jnp.dot(emat[g], side, preferred_element_type=F32)
        width = both.shape[1] // 2
        return both[:, :width] + both[:, width:]

    def at(ref, g):
        return ref[pl.ds(g * face, face)].reshape(frows, ref.shape[-1])

    def put(ref, g, value):
        ref[pl.ds(g * face, face)] = value.reshape(face, blk, value.shape[-1])

    width = ybuf.shape[-1]

    def load_side(source):
        for b in range(nblk):
            t, r = b // per, b % per
            vb[r * blk:(r + 1) * blk, t * width:(t + 1) * width] = source[inv_ref[b]].astype(BF16)

    def product(g):
        pieces, blocks = [], []
        for k in range(face):
            b = slot_ref[g * face + k]
            pieces.append(ops[b])
            blocks.append(jnp.broadcast_to(b, (blk, width)))
        wide = jnp.dot(jnp.concatenate(pieces, axis=0), vb[...], preferred_element_type=F32)
        block = jnp.concatenate(blocks, axis=0)
        value = wide[:, :width]
        for t in range(1, parts):
            value = jnp.where(block >= t * per, wide[:, t * width:(t + 1) * width], value)
        return value

    def start_halo(f):
        there, _, landing = partner(f)

        @pl.when(there)
        def _():
            halo_copy(f, landing).start()

    def wait_halo():
        for f in (0, 1, 2, 3):
            there, _, _ = partner(f)

            @pl.when(there)
            def _():
                halo_copy(f, f).wait_recv()

    def wait_halo_sent():
        for f in range(4):
            there, _, _ = partner(f)

            @pl.when(there)
            def _():
                halo_copy(f, f).wait_send()

    def assembled(g):
        mine = at(ybuf, g)
        if g < 4:
            return mine - halo[g].reshape(frows, width)
        if g < 6:
            return mine
        return mine - at(ybuf, 13 - g)

    def terms_of(g, value):
        high, low = split(value)
        return jnp.dot(mhl[g], jnp.concatenate([high, low], axis=1), preferred_element_type=F32)

    def fold(both):
        return both[:unit, :width] + (both[:unit, width:] + both[unit:, :width])

    def weight(g):
        if g < 4:
            there, _, _ = partner(g)
            return jnp.where(there, 0.5, 1.0).astype(F32)
        return 1.0 if g < 6 else 0.5

    def gather(par, terms):
        hall[par, c, i] = terms
        zs, ss = [], []
        for k in range(1, nc):
            zs.append(pltpu.make_async_remote_copy(
                src_ref=hall.at[par, c, i], dst_ref=hall.at[par, c, i],
                send_sem=zsend.at[k], recv_sem=zrecv.at[par, c],
                device_id=(lax.rem(c + k, nc), i), device_id_type=MESH))
        for copy in zs:
            copy.start()
        for k in range(1, nc):
            peer = lax.rem(c + k, nc)
            pltpu.make_async_remote_copy(
                src_ref=hall.at[par, peer, i], dst_ref=hall.at[par, peer, i],
                send_sem=zsend.at[k], recv_sem=zrecv.at[par, peer],
                device_id=(peer, i), device_id_type=MESH).wait_recv()
        for k in range(1, ns):
            ss.append(pltpu.make_async_remote_copy(
                src_ref=hall.at[par, :, i], dst_ref=hall.at[par, :, i],
                send_sem=ssend.at[k], recv_sem=srecv.at[par, i],
                device_id=(c, lax.rem(i + k, ns)), device_id_type=MESH))
        for copy in ss:
            copy.start()
        for k in range(1, ns):
            peer = lax.rem(i + k, ns)
            pltpu.make_async_remote_copy(
                src_ref=hall.at[par, :, peer], dst_ref=hall.at[par, :, peer],
                send_sem=ssend.at[k], recv_sem=srecv.at[par, peer],
                device_id=(c, peer), device_id_type=MESH).wait_recv()
        for copy in zs + ss:
            copy.wait_send()
        whole = hall[par].reshape(nc * ns, unit, width)
        return jnp.sum(whole, axis=0), coarse(whole.reshape(nc * ns * unit, width))

    def total(value):
        gz[c] = value
        zs, ss = [], []
        for k in range(1, nc):
            zs.append(pltpu.make_async_remote_copy(
                src_ref=gz.at[c], dst_ref=gz.at[c], send_sem=zsend.at[k], recv_sem=gzrecv.at[c],
                device_id=(lax.rem(c + k, nc), i), device_id_type=MESH))
        for copy in zs:
            copy.start()
        for k in range(1, nc):
            peer = lax.rem(c + k, nc)
            pltpu.make_async_remote_copy(
                src_ref=gz.at[peer], dst_ref=gz.at[peer], send_sem=zsend.at[k], recv_sem=gzrecv.at[peer],
                device_id=(peer, i), device_id_type=MESH).wait_recv()
        gs[i] = jnp.sum(gz[...], axis=0)
        for k in range(1, ns):
            ss.append(pltpu.make_async_remote_copy(
                src_ref=gs.at[i], dst_ref=gs.at[i], send_sem=ssend.at[k], recv_sem=gsrecv.at[i],
                device_id=(c, lax.rem(i + k, ns)), device_id_type=MESH))
        for copy in ss:
            copy.start()
        for k in range(1, ns):
            peer = lax.rem(i + k, ns)
            pltpu.make_async_remote_copy(
                src_ref=gs.at[peer], dst_ref=gs.at[peer], send_sem=ssend.at[k], recv_sem=gsrecv.at[peer],
                device_id=(c, peer), device_id_type=MESH).wait_recv()
        for copy in zs + ss:
            copy.wait_send()
        return jnp.sum(jnp.sum(gs[...], axis=0), axis=0, keepdims=True)

    row_ids = lax.broadcasted_iota(jnp.int32, (unit, width), 0)

    side = spread_side(coarse(cload_ref[...]))
    for g in range(8):
        put(mult, g, correct(g, side))
    load_side(mult)
    loads_copy.wait()
    ops_copy.wait()

    def loads_at(g):
        return jnp.concatenate([proj[slot_ref[g * face + k]] for k in range(face)], axis=0)

    def first_outer(step, carry):
        f = (step + 2) % 4
        put(ybuf, f, loads_at(f) - product(f))
        start_halo(f)
        return carry

    def first_inner(g, carry):
        put(ybuf, g, loads_at(g) - product(g))
        return carry

    lax.fori_loop(0, 4, first_outer, 0)
    lax.fori_loop(4, 8, first_inner, 0)
    terms = jnp.zeros((2 * unit, 2 * width), F32)
    wait_halo()
    for g in (4, 5, 6, 7, 0, 1, 2, 3):
        value = assembled(g)
        put(res, g, value)
        terms = terms + terms_of(g, value)
    wait_halo_sent()
    _, coeff = gather(0, fold(terms))
    side = spread_side(coeff)
    part = jnp.zeros((8, width), F32)
    for g in range(8):
        value = at(res, g) - correct(g, side)
        put(dire, g, value)
        part = part + weight(g) * rows8(value * value)
    gamma = None

    for iteration in range(ITERS):
        load_side(dire)

        def outer(step, carry):
            f = (step + 2) % 4
            value = product(f)
            put(ybuf, f, value)
            start_halo(f)
            return carry + rows8(value * at(dire, f))

        def inner(g, carry):
            value = product(g)
            put(ybuf, g, value)
            return carry + rows8(value * at(dire, g))

        curv = lax.fori_loop(0, 4, outer, jnp.zeros((8, width), F32))
        curv = lax.fori_loop(4, 8, inner, curv)
        curv = jnp.sum(curv, axis=0, keepdims=True)
        terms = jnp.zeros((2 * unit, 2 * width), F32)
        wait_halo()
        for g in (4, 5, 6, 7, 0, 1, 2, 3):
            value = assembled(g)
            put(img, g, value)
            terms = terms + terms_of(g, value)
        wait_halo_sent()
        message = jnp.where(row_ids == PAD - 2, curv, fold(terms))
        if gamma is None:
            message = jnp.where(row_ids == PAD - 1, jnp.sum(part, axis=0, keepdims=True), message)
        sums, coeff_image = gather((iteration + 1) % 2, message)
        if gamma is None:
            gamma = sums[PAD - 1:PAD]
        length = gamma / sums[PAD - 2:PAD - 1]
        coeff = coeff - length * coeff_image
        side = spread_side(coeff)
        last = iteration + 1 == ITERS
        part = jnp.zeros((8, width), F32)
        for g in range(8):
            put(mult, g, at(mult, g) + length * at(dire, g))
            value = at(res, g) - length * at(img, g)
            if not last:
                put(res, g, value)
            value = value - correct(g, side)
            put(proj, g, value)
            if not last:
                part = part + weight(g) * rows8(value * value)
        if not last:
            following = total(part)
            ratio = following / gamma
            gamma = following
            for g in range(8):
                put(dire, g, at(proj, g) + ratio * at(dire, g))

    for b in range(nblk):
        mult_out[b] = mult[inv_ref[b]]
        proj_out[b] = proj[inv_ref[b]]


def solution(mesh):
    nc, ns = mesh.shape["cluster"], mesh.shape["sub"]
    devices = nc * ns

    def on_device(dual_operators, local_loads, modes, coarse_matrix, coarse_loads, slot_block):
        parts, order, loads = local_loads.shape
        nmode = modes.shape[1]
        slots = slot_block[0]
        nblk = slots.shape[0]
        face = nblk // 8
        blk = order * parts // nblk
        unit = parts * PAD
        positions = jnp.arange(nblk, dtype=jnp.int32)
        inverse = jnp.sum(
            positions[:, None] * (slots[:, None] == positions[None, :]).astype(jnp.int32), axis=0)
        extra = PAD - nmode
        per = nblk // parts
        modes8 = jnp.pad(
            modes.reshape(parts, nmode, per, blk).transpose(0, 2, 1, 3).reshape(nblk, nmode, blk),
            ((0, 0), (0, extra), (0, 0)))
        cmat = jnp.pad(
            coarse_matrix.reshape(parts, nmode, devices * parts, nmode),
            ((0, 0), (0, extra), (0, 0), (0, extra))).reshape(unit, devices * unit)
        cload = jnp.pad(
            coarse_loads.reshape(devices * parts, nmode, loads),
            ((0, 0), (0, extra), (0, 0))).reshape(devices * unit, loads)
        vmem = pl.BlockSpec(memory_space=pltpu.VMEM)
        smem = pl.BlockSpec(memory_space=pltpu.SMEM)
        anym = pl.BlockSpec(memory_space=pl.ANY)
        vec = pltpu.VMEM((nblk, blk, loads), F32)
        dma = pltpu.SemaphoreType.DMA
        out = jax.ShapeDtypeStruct((nblk, blk, loads), F32)
        mult, proj = pl.pallas_call(
            functools.partial(kernel, nc, ns, parts, face),
            out_shape=(out, out),
            in_specs=[smem, smem, anym, anym, vmem, vmem, vmem],
            out_specs=(vmem, vmem),
            scratch_shapes=[
                pltpu.VMEM((nblk, blk, order), BF16),
                vec, vec, vec, vec, vec, vec,
                pltpu.VMEM((8, face * blk, 2 * LANES), BF16),
                pltpu.VMEM((order, parts * loads), BF16),
                pltpu.VMEM((4, face, blk, loads), F32),
                pltpu.VMEM((nblk, unit, blk), F32),
                pltpu.VMEM((4, face, unit, blk), F32),
                pltpu.VMEM((8, 2 * unit, face * blk), BF16),
                pltpu.VMEM((5, unit, devices * unit), F32),
                pltpu.VMEM((2, nc, ns, unit, loads), F32),
                pltpu.VMEM((nc, 8, loads), F32),
                pltpu.VMEM((ns, 8, loads), F32),
                dma(()), dma(()),
                dma((4,)), dma((4,)), dma((4,)), dma((4,)), dma((4,)), dma((4,)),
                dma((nc,)), dma((2, nc)), dma((ns,)), dma((2, ns)), dma((nc,)), dma((ns,)),
            ],
            compiler_params=pltpu.CompilerParams(
                collective_id=0, has_side_effects=True, vmem_limit_bytes=56 * 1024 * 1024),
            cost_estimate=pl.CostEstimate(
                flops=8 * parts * order * order * loads, bytes_accessed=24 * 1024 * 1024, transcendentals=0),
        )(slots, inverse, dual_operators.reshape(nblk, blk, order), local_loads.reshape(nblk, blk, loads), modes8, cmat, cload)
        return mult.reshape(local_loads.shape), proj.reshape(local_loads.shape)

    return jax.shard_map(
        on_device,
        mesh=mesh,
        in_specs=(
            P(("cluster", "sub"), None, None),
            P(("cluster", "sub"), None, None),
            P(("cluster", "sub"), None, None),
            P(("cluster", "sub"), None),
            P(),
            P(("cluster", "sub"), None),
        ),
        out_specs=(P(("cluster", "sub"), None, None), P(("cluster", "sub"), None, None)),
        check_vma=False,
    )
```

time: 793 us -> 121 us (0.15); the launches traced: 781 us -> 121 us
  blocking collectives: 377 us -> 0 us
  starting transfers between devices: 110 us -> 0 us
  Pallas kernels: 0 us -> 109 us
  local copies, waits for them, and re-layouts: 108 us -> 9.87 us
  matrix products: 86.6 us -> 0 us
  other arithmetic: 72.7 us -> 1.33 us
  waiting for transfers between devices: 24.9 us -> 0 us
    psum x5 -> x0, blocking collectives: 207 us -> none  [the longest x3 120 us: residual_norm(): return lax.psum(inner_product(values, values), ('cluster', 'sub'))]
    all_gather x4 -> x0, blocking collectives: 170 us -> none  [coarse_coefficients(): lax.all_gather(coarse_terms, ('cluster', 'sub'), axis=0, tiled=True)]
    ppermute x44 -> x0, starting transfers between devices: 110 us -> none  [the longest x24 56.2 us: from_behind(): lax.ppermute(value, axis, [(source, source + steps) for source in range(i...]
    pallas_call x0 -> x1, Pallas kernels: none -> 109 us  [on_device(): pl.pallas_call(functools.partial(kernel, nc, ns, parts, face), out_shape=...]
    dot_general x28 -> x0, matrix products: 86.6 us -> none  [the longest x4 52 us: apply_dual(): jnp.einsum('smn,snl->sml', dual_operators, direction.astype(jnp.bfloat16)...]
    gather x22 -> x0, local copies, waits for them, and re-layouts: 65.2 us -> none  [the longest x10 34.8 us: from_slots(): slot_values[inverse].reshape(local_count, dual_order, slot_values.shape[-1])]
    sub x16 -> x0, other arithmetic: 40.8 us -> none  [the longest x5 12.9 us: correct(): return from_slots(own_part - partner_part)]
    ppermute x44 -> x0, waiting for transfers between devices: 24.9 us -> none  [the longest x24 21.5 us: from_behind(): lax.ppermute(value, axis, [(source, source + steps) for source in range(i...]
  transfers between devices with their start and end apart: 44 -> 0, of which waited for: 11 -> 0; matrix products, arithmetic and copies ran while one was open for 12% -> 0% of each run, Pallas kernels for 0% -> 0%
where the time goes in v1:
time: 121 us
  Pallas kernels  109 us (90%)
  local copies, waits for them, and re-layouts  9.87 us (8%)
  other arithmetic  1.33 us (1%)
    pallas_call x1, Pallas kernels, on_device(): pl.pallas_call(functools.partial(kernel, nc, ns, parts, face), out_shape=...  109 us
    unnamed x4, local copies, waits for them, and re-layouts  4.52 us

profile of v1, /device:TPU:0, one launch (start us, length us, event | category | flops | bytes accessed | tf_op | source)
XLA Modules:
  0.0 120.7 jit_solution(15854082069723651741)
XLA Ops:
  0.6 1.3 %select_reduce_fusion.inv_ref = s32[32]{0:T(128)} fusion(s32[32]{0:T(128)} %bitcast.19), kind=kLoop, calls=%fused_computation.1 | loop fusion | flops 3040 | bytes 256 | tf_op jit(solution)/shard_map/reduce_sum | solution.py:399
  2.0 1.0 reshape.37
  2.9 0.1 copy.10
  3.0 0.7 pad.12.modes_ref
  3.7 1.0 reshape.41
  4.6 0.7 pad_bitcast_fusion.cload_ref
  5.4 1.1 reshape.39
  6.5 0.9 reshape.40.cmat_ref
  7.3 108.8 %shard_map.77 = (f32[32,128,128]{2,1,0:T(8,128)}, f32[32,128,128]{2,1,0:T(8,128)}) custom-call(s32[32]{0:T(128)} %bitcast.20, s32[32]{0:T(128)} %select_reduce_fusion.inv_ref, bf16[32,128,2048]{2,1,0:T(8,128)(2,1)} %bitcast.17, f32[32,128,128]{2,1,0:T(8,128)} %bitcast.18, f32[32,8,128]{2,1,0:T(8,128)} %pad.12.modes_ref, f32[16,512]{1,0:T(8,128)} %reshape.40.cmat_ref, ...), custom_call_target="tpu_custom_call" | custom-call | flops 8589934592 | bytes 25165824 | tf_op jit(solution)/shard_map/pallas_call | solution.py:418
  116.2 0.0 copy-start
  116.2 3.2 %copy.13 = f32[2,2048,128]{2,1,0:T(8,128)} copy(f32[2,2048,128]{2,1,0:T(8,128)} %bitcast.15) | data formatting | bytes 4194304
  119.4 0.0 copy-done
  119.4 1.3 %copy.14 = f32[2,2048,128]{2,1,0:T(8,128)} copy(f32[2,2048,128]{2,1,0:T(8,128)S(1)} %bitcast.14) | data formatting | bytes 4194304
  (1 shorter events, 0.0 us)
Async XLA Ops:
  116.2 3.2 %copy-start = (f32[32,128,128]{2,1,0:T(8,128)S(1)}, f32[32,128,128]{2,1,0:T(8,128)}, u32[]{:S(2)}) copy-start(f32[32,128,128]{2,1,0:T(8,128)} %get-tuple-element.5) | copy-start | bytes 6291460

commit v2 on v1

--- a/solution.py
+++ b/solution.py
@@ -27,7 +27,7 @@
     nc, ns, parts, face,
     slot_ref, inv_ref, ops_hbm, loads_hbm, modes_ref, cmat_ref, cload_ref,
     mult_out, proj_out,
-    ops, ybuf, img, res, proj, dire, mult, emat, vb, halo, mslot, mfetch, mhl, call, hall, gz, gs,
+    ops, ybuf, res, proj, dire, mult, emat, vb, halo, mraw, mslot, mfetch, mhl, call, cpad, hall, gz, gs,
     ops_sem, loads_sem, halo_send, halo_recv, m_send, m_recv, c_send, c_recv,
     zsend, zrecv, ssend, srecv, gzrecv, gsrecv,
 ):
@@ -37,9 +37,15 @@
     blk = ybuf.shape[1]
     frows = face * blk
     unit = parts * PAD
-
-    ops_copy = pltpu.make_async_copy(ops_hbm, ops, ops_sem)
-    ops_copy.start()
+    width = ybuf.shape[-1]
+
+    nmode = modes_ref.shape[1]
+    ops_copies = [
+        pltpu.make_async_copy(
+            ops_hbm.at[pl.ds(k * face, face)], ops.at[pl.ds(k * face, face)], ops_sem.at[k])
+        for k in range(8)]
+    for copy in ops_copies:
+        copy.start()
     loads_copy = pltpu.make_async_copy(loads_hbm, proj, loads_sem)
     loads_copy.start()
 
@@ -49,14 +55,20 @@
     for k in range(1, ns):
         pl.semaphore_signal(barrier, inc=1, device_id=(c, lax.rem(i + k, ns)), device_id_type=MESH)
 
+    mraw[...] = jnp.zeros_like(mraw)
+    for b in range(nblk):
+        t, r = b // per, b % per
+        mraw[b, 0:nmode, :] = modes_ref[t, :, r * blk:(r + 1) * blk]
     for j in range(nblk):
-        b = slot_ref[j]
-        piece = modes_ref[b]
+        b = slot_ref[0, j]
+        piece = mraw[b]
         block = jnp.broadcast_to(b, piece.shape)
         for own in range(parts):
             mine = (block >= own * per) & (block < (own + 1) * per)
             mslot[j, own * PAD:(own + 1) * PAD, :] = jnp.where(mine, piece, 0.0)
-    call[0] = cmat_ref[...]
+    call[0] = jnp.zeros(call.shape[1:], F32)
+    for t in range(parts):
+        call[0, t * PAD:t * PAD + nmode, :] = cmat_ref[t * nmode:(t + 1) * nmode, :]
 
     def partner(f):
         axis, sign = f // 2, 2 * (f % 2) - 1
@@ -64,11 +76,11 @@
         there = (tc >= 0) & (tc < nc) & (ti >= 0) & (ti < ns)
         return there, (tc, ti), axis * 2 + 1 - f % 2
 
-    def halo_copy(f, landing):
+    def halo_copy(f, landing, par):
         _, device, _ = partner(f)
         return pltpu.make_async_remote_copy(
-            src_ref=ybuf.at[pl.ds(f * face, face)], dst_ref=halo.at[landing],
-            send_sem=halo_send.at[f], recv_sem=halo_recv.at[landing],
+            src_ref=ybuf.at[pl.ds(f * face, face)], dst_ref=halo.at[par, landing],
+            send_sem=halo_send.at[f], recv_sem=halo_recv.at[par, landing],
             device_id=device, device_id_type=MESH)
 
     def mode_copy(f, landing):
@@ -96,13 +108,20 @@
 
         @pl.when(jnp.logical_not(there))
         def _():
-            halo[f] = jnp.zeros(halo.shape[1:], F32)
+            halo[0, f] = jnp.zeros(halo.shape[2:], F32)
+            halo[1, f] = jnp.zeros(halo.shape[2:], F32)
             mfetch[f] = jnp.zeros(mfetch.shape[1:], F32)
             call[f + 1] = jnp.zeros(call.shape[1:], F32)
 
     for g in range(8):
         for k in range(face):
-            high, low = split(mslot[g * face + k])
+            j = g * face + k
+            own = mslot[j]
+            if g == 6:
+                own = own - mslot[j + face]
+            if g == 7:
+                own = own - mslot[j - face]
+            high, low = split(own)
             mhl[g, 0:unit, k * blk:(k + 1) * blk] = high
             mhl[g, unit:2 * unit, k * blk:(k + 1) * blk] = low
 
@@ -135,10 +154,29 @@
             emat[g, k * blk:(k + 1) * blk, 0:LANES] = high
             emat[g, k * blk:(k + 1) * blk, LANES:] = low
 
+    highest = lax.Precision.HIGHEST
     cfull = call[...].reshape(5 * unit, call.shape[-1])
+    first = jnp.dot(cfull, cload_ref[...], precision=highest, preferred_element_type=F32)
+    columns = call.shape[-1]
+    chunk = nmode * LANES // 2
+    if columns % chunk:
+        chunk = columns
+    padded = chunk // nmode * PAD
+    place_rows = lax.broadcasted_iota(jnp.int32, (chunk, padded), 0)
+    place_cols = lax.broadcasted_iota(jnp.int32, (chunk, padded), 1)
+    group, mode = place_cols >> 3, place_cols & (PAD - 1)
+    place = jnp.where((place_rows == group * nmode + mode) & (mode < nmode), 1.0, 0.0).astype(F32)
+    for k in range(columns // chunk):
+        high, low = split(jnp.dot(
+            cfull[:, k * chunk:(k + 1) * chunk], place, precision=highest, preferred_element_type=F32))
+        cpad[0:5 * unit, k * padded:(k + 1) * padded] = high
+        cpad[5 * unit:10 * unit, k * padded:(k + 1) * padded] = low
 
     def coarse(terms):
-        return jnp.dot(cfull, terms, precision=lax.Precision.HIGHEST, preferred_element_type=F32)
+        high, low = split(terms)
+        both = jnp.dot(cpad[...], jnp.concatenate([high, low], axis=1), preferred_element_type=F32)
+        top = 5 * unit
+        return both[:top, :width] + (both[:top, width:] + both[top:, :width])
 
     def spread_side(coeff):
         high, low = split(jnp.concatenate(
@@ -158,8 +196,6 @@
     def put(ref, g, value):
         ref[pl.ds(g * face, face)] = value.reshape(face, blk, value.shape[-1])
 
-    width = ybuf.shape[-1]
-
     def load_side(source):
         for b in range(nblk):
             t, r = b // per, b % per
@@ -168,7 +204,7 @@
     def product(g):
         pieces, blocks = [], []
         for k in range(face):
-            b = slot_ref[g * face + k]
+            b = slot_ref[0, g * face + k]
             pieces.append(ops[b])
             blocks.append(jnp.broadcast_to(b, (blk, width)))
         wide = jnp.dot(jnp.concatenate(pieces, axis=0), vb[...], preferred_element_type=F32)
@@ -178,33 +214,32 @@
             value = jnp.where(block >= t * per, wide[:, t * width:(t + 1) * width], value)
         return value
 
-    def start_halo(f):
+    def start_halo(f, par):
         there, _, landing = partner(f)
 
         @pl.when(there)
         def _():
-            halo_copy(f, landing).start()
-
-    def wait_halo():
-        for f in (0, 1, 2, 3):
+            halo_copy(f, landing, par).start()
+
+    def wait_halo(f, par):
+        there, _, _ = partner(f)
+
+        @pl.when(there)
+        def _():
+            halo_copy(f, f, par).wait_recv()
+
+    def wait_halo_sent(par):
+        for f in range(4):
             there, _, _ = partner(f)
 
             @pl.when(there)
             def _():
-                halo_copy(f, f).wait_recv()
-
-    def wait_halo_sent():
-        for f in range(4):
-            there, _, _ = partner(f)
-
-            @pl.when(there)
-            def _():
-                halo_copy(f, f).wait_send()
-
-    def assembled(g):
+                halo_copy(f, f, par).wait_send()
+
+    def assembled(g, par):
         mine = at(ybuf, g)
         if g < 4:
-            return mine - halo[g].reshape(frows, width)
+            return mine - halo[par, g].reshape(frows, width)
         if g < 6:
             return mine
         return mine - at(ybuf, 13 - g)
@@ -212,6 +247,15 @@
     def terms_of(g, value):
         high, low = split(value)
         return jnp.dot(mhl[g], jnp.concatenate([high, low], axis=1), preferred_element_type=F32)
+
+    def image_terms(par):
+        terms = lax.fori_loop(
+            0, 8, lambda g, carry: carry + terms_of(g, at(ybuf, g)),
+            jnp.zeros((2 * unit, 2 * width), F32))
+        for f in range(4):
+            wait_halo(f, par)
+            terms = terms - terms_of(f, halo[par, f].reshape(frows, width))
+        return terms
 
     def fold(both):
         return both[:unit, :width] + (both[:unit, width:] + both[unit:, :width])
@@ -256,7 +300,7 @@
         whole = hall[par].reshape(nc * ns, unit, width)
         return jnp.sum(whole, axis=0), coarse(whole.reshape(nc * ns * unit, width))
 
-    def total(value):
+    def total(value, meanwhile):
         gz[c] = value
         zs, ss = [], []
         for k in range(1, nc):
@@ -265,6 +309,7 @@
                 device_id=(lax.rem(c + k, nc), i), device_id_type=MESH))
         for copy in zs:
             copy.start()
+        meanwhile()
         for k in range(1, nc):
             peer = lax.rem(c + k, nc)
             pltpu.make_async_remote_copy(
@@ -288,20 +333,21 @@
 
     row_ids = lax.broadcasted_iota(jnp.int32, (unit, width), 0)
 
-    side = spread_side(coarse(cload_ref[...]))
+    side = spread_side(first)
     for g in range(8):
         put(mult, g, correct(g, side))
     load_side(mult)
     loads_copy.wait()
-    ops_copy.wait()
+    for copy in ops_copies:
+        copy.wait()
 
     def loads_at(g):
-        return jnp.concatenate([proj[slot_ref[g * face + k]] for k in range(face)], axis=0)
+        return jnp.concatenate([proj[slot_ref[0, g * face + k]] for k in range(face)], axis=0)
 
     def first_outer(step, carry):
         f = (step + 2) % 4
         put(ybuf, f, loads_at(f) - product(f))
-        start_halo(f)
+        start_halo(f, 0)
         return carry
 
     def first_inner(g, carry):
@@ -310,30 +356,28 @@
 
     lax.fori_loop(0, 4, first_outer, 0)
     lax.fori_loop(4, 8, first_inner, 0)
-    terms = jnp.zeros((2 * unit, 2 * width), F32)
-    wait_halo()
-    for g in (4, 5, 6, 7, 0, 1, 2, 3):
-        value = assembled(g)
-        put(res, g, value)
-        terms = terms + terms_of(g, value)
-    wait_halo_sent()
-    _, coeff = gather(0, fold(terms))
+    _, coeff = gather(0, fold(image_terms(0)))
+    wait_halo_sent(0)
     side = spread_side(coeff)
     part = jnp.zeros((8, width), F32)
     for g in range(8):
-        value = at(res, g) - correct(g, side)
+        value = assembled(g, 0)
+        put(res, g, value)
+        value = value - correct(g, side)
         put(dire, g, value)
         part = part + weight(g) * rows8(value * value)
     gamma = None
 
     for iteration in range(ITERS):
+        par = (iteration + 1) % 2
+        last = iteration + 1 == ITERS
         load_side(dire)
 
         def outer(step, carry):
             f = (step + 2) % 4
             value = product(f)
             put(ybuf, f, value)
-            start_halo(f)
+            start_halo(f, par)
             return carry + rows8(value * at(dire, f))
 
         def inner(g, carry):
@@ -344,43 +388,40 @@
         curv = lax.fori_loop(0, 4, outer, jnp.zeros((8, width), F32))
         curv = lax.fori_loop(4, 8, inner, curv)
         curv = jnp.sum(curv, axis=0, keepdims=True)
-        terms = jnp.zeros((2 * unit, 2 * width), F32)
-        wait_halo()
-        for g in (4, 5, 6, 7, 0, 1, 2, 3):
-            value = assembled(g)
-            put(img, g, value)
-            terms = terms + terms_of(g, value)
-        wait_halo_sent()
-        message = jnp.where(row_ids == PAD - 2, curv, fold(terms))
+        message = jnp.where(row_ids == PAD - 2, curv, fold(image_terms(par)))
         if gamma is None:
             message = jnp.where(row_ids == PAD - 1, jnp.sum(part, axis=0, keepdims=True), message)
-        sums, coeff_image = gather((iteration + 1) % 2, message)
+        sums, coeff_image = gather(par, message)
+        wait_halo_sent(par)
         if gamma is None:
             gamma = sums[PAD - 1:PAD]
         length = gamma / sums[PAD - 2:PAD - 1]
         coeff = coeff - length * coeff_image
         side = spread_side(coeff)
-        last = iteration + 1 == ITERS
         part = jnp.zeros((8, width), F32)
         for g in range(8):
-            put(mult, g, at(mult, g) + length * at(dire, g))
-            value = at(res, g) - length * at(img, g)
+            value = at(res, g) - length * assembled(g, par)
             if not last:
                 put(res, g, value)
             value = value - correct(g, side)
             put(proj, g, value)
             if not last:
                 part = part + weight(g) * rows8(value * value)
-        if not last:
-            following = total(part)
+        if last:
+            for b in range(nblk):
+                s = inv_ref[b]
+                mult_out[b] = mult[s] + length * dire[s]
+                proj_out[b] = proj[s]
+        else:
+            def step_multipliers():
+                for g in range(8):
+                    put(mult, g, at(mult, g) + length * at(dire, g))
+
+            following = total(part, step_multipliers)
             ratio = following / gamma
             gamma = following
             for g in range(8):
                 put(dire, g, at(proj, g) + ratio * at(dire, g))
-
-    for b in range(nblk):
-        mult_out[b] = mult[inv_ref[b]]
-        proj_out[b] = proj[inv_ref[b]]
 
 
 def solution(mesh):
@@ -398,17 +439,6 @@
         positions = jnp.arange(nblk, dtype=jnp.int32)
         inverse = jnp.sum(
             positions[:, None] * (slots[:, None] == positions[None, :]).astype(jnp.int32), axis=0)
-        extra = PAD - nmode
-        per = nblk // parts
-        modes8 = jnp.pad(
-            modes.reshape(parts, nmode, per, blk).transpose(0, 2, 1, 3).reshape(nblk, nmode, blk),
-            ((0, 0), (0, extra), (0, 0)))
-        cmat = jnp.pad(
-            coarse_matrix.reshape(parts, nmode, devices * parts, nmode),
-            ((0, 0), (0, extra), (0, 0), (0, extra))).reshape(unit, devices * unit)
-        cload = jnp.pad(
-            coarse_loads.reshape(devices * parts, nmode, loads),
-            ((0, 0), (0, extra), (0, 0))).reshape(devices * unit, loads)
         vmem = pl.BlockSpec(memory_space=pltpu.VMEM)
         smem = pl.BlockSpec(memory_space=pltpu.SMEM)
         anym = pl.BlockSpec(memory_space=pl.ANY)
@@ -422,26 +452,29 @@
             out_specs=(vmem, vmem),
             scratch_shapes=[
                 pltpu.VMEM((nblk, blk, order), BF16),
-                vec, vec, vec, vec, vec, vec,
+                vec, vec, vec, vec, vec,
                 pltpu.VMEM((8, face * blk, 2 * LANES), BF16),
                 pltpu.VMEM((order, parts * loads), BF16),
-                pltpu.VMEM((4, face, blk, loads), F32),
+                pltpu.VMEM((2, 4, face, blk, loads), F32),
+                pltpu.VMEM((nblk, PAD, blk), F32),
                 pltpu.VMEM((nblk, unit, blk), F32),
                 pltpu.VMEM((4, face, unit, blk), F32),
                 pltpu.VMEM((8, 2 * unit, face * blk), BF16),
-                pltpu.VMEM((5, unit, devices * unit), F32),
+                pltpu.VMEM((5, unit, coarse_matrix.shape[1]), F32),
+                pltpu.VMEM((10 * unit, devices * unit), BF16),
                 pltpu.VMEM((2, nc, ns, unit, loads), F32),
                 pltpu.VMEM((nc, 8, loads), F32),
                 pltpu.VMEM((ns, 8, loads), F32),
-                dma(()), dma(()),
-                dma((4,)), dma((4,)), dma((4,)), dma((4,)), dma((4,)), dma((4,)),
+                dma((8,)), dma(()),
+                dma((4,)), dma((2, 4)), dma((4,)), dma((4,)), dma((4,)), dma((4,)),
                 dma((nc,)), dma((2, nc)), dma((ns,)), dma((2, ns)), dma((nc,)), dma((ns,)),
             ],
             compiler_params=pltpu.CompilerParams(
                 collective_id=0, has_side_effects=True, vmem_limit_bytes=56 * 1024 * 1024),
             cost_estimate=pl.CostEstimate(
                 flops=8 * parts * order * order * loads, bytes_accessed=24 * 1024 * 1024, transcendentals=0),
-        )(slots, inverse, dual_operators.reshape(nblk, blk, order), local_loads.reshape(nblk, blk, loads), modes8, cmat, cload)
+        )(slot_block, inverse, dual_operators.reshape(nblk, blk, order),
+          local_loads.reshape(nblk, blk, loads), modes, coarse_matrix, coarse_loads)
         return mult.reshape(local_loads.shape), proj.reshape(local_loads.shape)
 
     return jax.shard_map(

time: 121 us -> 116 us (0.959)
  local copies, waits for them, and re-layouts: 9.87 us -> 6.13 us
  Pallas kernels: 109 us -> 107 us
    reshape x6 -> x0, local copies, waits for them, and re-layouts: 4.65 us -> none  [the longest x1 1.08 us: on_device(): coarse_matrix.reshape(parts, nmode, devices * parts, nmode)]
    unnamed x4 -> x5, local copies, waits for them, and re-layouts: 4.52 us -> 6.13 us
    pallas_call x1, Pallas kernels: 109 us -> 107 us  [on_device(): pl.pallas_call(functools.partial(kernel, nc, ns, parts, face), out_shape=...]
where the time goes in v2:
time: 116 us; the launch traced here: 115 us
  Pallas kernels  107 us (92%)
  local copies, waits for them, and re-layouts  6.13 us (5%)
  other arithmetic  1.25 us (1%)
    pallas_call x1, Pallas kernels, on_device(): pl.pallas_call(functools.partial(kernel, nc, ns, parts, face), out_shape=...  107 us
    unnamed x5, local copies, waits for them, and re-layouts  6.13 us

profile of v2, /device:TPU:0, one launch (start us, length us, event | category | flops | bytes accessed | tf_op | source)
XLA Modules:
  0.0 115.5 jit_solution(14255463206868760006)
XLA Ops:
  0.6 1.3 %select_reduce_fusion.inv_ref = s32[32]{0:T(128)} fusion(s32[32]{0:T(128)} %bitcast.9), kind=kLoop, calls=%fused_computation | loop fusion | flops 3040 | bytes 256 | tf_op jit(solution)/shard_map/reduce_sum | solution.py:440
  1.9 1.6 %copy.9.modes_ref = f32[2,6,2048]{2,1,0:T(8,128)} copy(f32[2,6,2048]{2,0,1:T(2,128)} %param.8) | data formatting | bytes 196608 | tf_op args[2]
  3.5 107.4 %shard_map.77 = (f32[32,128,128]{2,1,0:T(8,128)}, f32[32,128,128]{2,1,0:T(8,128)}) custom-call(s32[1,32]{1,0:T(1,128)} %slot_ref.1, s32[32]{0:T(128)} %select_reduce_fusion.inv_ref, bf16[32,128,2048]{2,1,0:T(8,128)(2,1)} %bitcast.7, f32[32,128,128]{2,1,0:T(8,128)} %bitcast.8, f32[2,6,2048]{2,1,0:T(8,128)} %copy.9.modes_ref, f32[12,384]{1,0:T(8,128)} %cmat_ref.1, ...), custom_call_target="tpu_custom_call" | custom-call | flops 8589934592 | bytes 25165824 | tf_op jit(solution)/shard_map/pallas_call | solution.py:448
  110.9 0.0 copy-start
  111.0 3.2 %copy.12 = f32[2,2048,128]{2,1,0:T(8,128)} copy(f32[2,2048,128]{2,1,0:T(8,128)} %bitcast.6) | data formatting | bytes 4194304
  114.1 0.0 copy-done
  114.1 1.3 %copy.13 = f32[2,2048,128]{2,1,0:T(8,128)} copy(f32[2,2048,128]{2,1,0:T(8,128)S(1)} %bitcast.5) | data formatting | bytes 4194304
Async XLA Ops:
  110.9 3.2 %copy-start = (f32[32,128,128]{2,1,0:T(8,128)S(1)}, f32[32,128,128]{2,1,0:T(8,128)}, u32[]{:S(2)}) copy-start(f32[32,128,128]{2,1,0:T(8,128)} %get-tuple-element.5) | copy-start | bytes 6291460

commit v3 on v2

--- a/solution.py
+++ b/solution.py
@@ -26,7 +26,7 @@
 def kernel(
     nc, ns, parts, face,
     slot_ref, inv_ref, ops_hbm, loads_hbm, modes_ref, cmat_ref, cload_ref,
-    mult_out, proj_out,
+    out_ref,
     ops, ybuf, res, proj, dire, mult, emat, vb, halo, mraw, mslot, mfetch, mhl, call, cpad, hall, gz, gs,
     ops_sem, loads_sem, halo_send, halo_recv, m_send, m_recv, c_send, c_recv,
     zsend, zrecv, ssend, srecv, gzrecv, gsrecv,
@@ -39,7 +39,7 @@
     unit = parts * PAD
     width = ybuf.shape[-1]
 
-    nmode = modes_ref.shape[1]
+    nmode = modes_ref.shape[0]
     ops_copies = [
         pltpu.make_async_copy(
             ops_hbm.at[pl.ds(k * face, face)], ops.at[pl.ds(k * face, face)], ops_sem.at[k])
@@ -58,7 +58,8 @@
     mraw[...] = jnp.zeros_like(mraw)
     for b in range(nblk):
         t, r = b // per, b % per
-        mraw[b, 0:nmode, :] = modes_ref[t, :, r * blk:(r + 1) * blk]
+        for m in range(nmode):
+            mraw[b, m:m + 1, :] = modes_ref[m, t:t + 1, r * blk:(r + 1) * blk]
     for j in range(nblk):
         b = slot_ref[0, j]
         piece = mraw[b]
@@ -207,7 +208,10 @@
             b = slot_ref[0, g * face + k]
             pieces.append(ops[b])
             blocks.append(jnp.broadcast_to(b, (blk, width)))
-        wide = jnp.dot(jnp.concatenate(pieces, axis=0), vb[...], preferred_element_type=F32)
+        rows = jnp.concatenate(pieces, axis=0)
+        half = rows.shape[1] // 2
+        wide = (jnp.dot(rows[:, :half], vb[:half], preferred_element_type=F32)
+                + jnp.dot(rows[:, half:], vb[half:], preferred_element_type=F32))
         block = jnp.concatenate(blocks, axis=0)
         value = wide[:, :width]
         for t in range(1, parts):
@@ -410,8 +414,8 @@
         if last:
             for b in range(nblk):
                 s = inv_ref[b]
-                mult_out[b] = mult[s] + length * dire[s]
-                proj_out[b] = proj[s]
+                out_ref[0, b] = mult[s] + length * dire[s]
+                out_ref[1, b] = proj[s]
         else:
             def step_multipliers():
                 for g in range(8):
@@ -444,12 +448,12 @@
         anym = pl.BlockSpec(memory_space=pl.ANY)
         vec = pltpu.VMEM((nblk, blk, loads), F32)
         dma = pltpu.SemaphoreType.DMA
-        out = jax.ShapeDtypeStruct((nblk, blk, loads), F32)
-        mult, proj = pl.pallas_call(
+        out = jax.ShapeDtypeStruct((2, nblk, blk, loads), F32)
+        both = pl.pallas_call(
             functools.partial(kernel, nc, ns, parts, face),
-            out_shape=(out, out),
+            out_shape=out,
             in_specs=[smem, smem, anym, anym, vmem, vmem, vmem],
-            out_specs=(vmem, vmem),
+            out_specs=vmem,
             scratch_shapes=[
                 pltpu.VMEM((nblk, blk, order), BF16),
                 vec, vec, vec, vec, vec,
@@ -474,8 +478,8 @@
             cost_estimate=pl.CostEstimate(
                 flops=8 * parts * order * order * loads, bytes_accessed=24 * 1024 * 1024, transcendentals=0),
         )(slot_block, inverse, dual_operators.reshape(nblk, blk, order),
-          local_loads.reshape(nblk, blk, loads), modes, coarse_matrix, coarse_loads)
-        return mult.reshape(local_loads.shape), proj.reshape(local_loads.shape)
+          local_loads.reshape(nblk, blk, loads), modes.transpose(1, 0, 2), coarse_matrix, coarse_loads)
+        return both[0].reshape(local_loads.shape), both[1].reshape(local_loads.shape)
 
     return jax.shard_map(
         on_device,

time: 116 us -> 114 us (0.983)
  local copies, waits for them, and re-layouts: 6.13 us -> 4.73 us
    unnamed x5 -> x0, local copies, waits for them, and re-layouts: 6.13 us -> none
    slice x0 -> x1, local copies, waits for them, and re-layouts: none -> 4.73 us  [on_device(): both[1].reshape(local_loads.shape)]
where the time goes in v3:
time: 114 us
  Pallas kernels  108 us (95%)
  local copies, waits for them, and re-layouts  4.73 us (4%)
  other arithmetic  1.25 us (1%)
    pallas_call x1, Pallas kernels, on_device(): pl.pallas_call(functools.partial(kernel, nc, ns, parts, face), out_shape=...  108 us
    slice x1, local copies, waits for them, and re-layouts, on_device(): both[1].reshape(local_loads.shape)  4.73 us

profile of v3, /device:TPU:0, one launch (start us, length us, event | category | flops | bytes accessed | tf_op | source)
XLA Modules:
  0.0 114.2 jit_solution(3972758484709329277)
XLA Ops:
  0.6 1.3 %select_reduce_fusion.inv_ref = s32[32]{0:T(128)} fusion(s32[32]{0:T(128)} %bitcast.11), kind=kLoop, calls=%fused_computation | loop fusion | flops 3040 | bytes 256 | tf_op jit(solution)/shard_map/reduce_sum | solution.py:444
  1.9 107.6 %shard_map.77 = f32[2,32,128,128]{3,2,1,0:T(8,128)} custom-call(s32[1,32]{1,0:T(1,128)} %slot_ref.1, s32[32]{0:T(128)} %select_reduce_fusion.inv_ref, bf16[32,128,2048]{2,1,0:T(8,128)(2,1)} %bitcast.8, f32[32,128,128]{2,1,0:T(8,128)} %bitcast.9, f32[6,2,2048]{2,1,0:T(2,128)} %bitcast.10, f32[12,384]{1,0:T(8,128)} %cmat_ref.1, f32[384,128]{1,0:T(8,128)} %cload_ref.1), custom_call_target="tpu_custom_call" | custom-call | flops 8589934592 | bytes 25165824 | tf_op jit(solution)/shard_map/pallas_call | solution.py:452
  109.5 4.7 %fusion = (f32[1,32,128,128]{3,2,1,0:T(8,128)}, f32[1,32,128,128]{3,2,1,0:T(8,128)}) fusion(f32[2,32,128,128]{3,2,1,0:T(8,128)} %shard_map.77), kind=kLoop, calls=%fused_computation.2 | loop fusion | bytes 8388608 | tf_op jit(solution)/shard_map/slice | solution.py:482

commit v4 on v3

--- a/solution.py
+++ b/solution.py
@@ -158,21 +158,6 @@
     highest = lax.Precision.HIGHEST
     cfull = call[...].reshape(5 * unit, call.shape[-1])
     first = jnp.dot(cfull, cload_ref[...], precision=highest, preferred_element_type=F32)
-    columns = call.shape[-1]
-    chunk = nmode * LANES // 2
-    if columns % chunk:
-        chunk = columns
-    padded = chunk // nmode * PAD
-    place_rows = lax.broadcasted_iota(jnp.int32, (chunk, padded), 0)
-    place_cols = lax.broadcasted_iota(jnp.int32, (chunk, padded), 1)
-    group, mode = place_cols >> 3, place_cols & (PAD - 1)
-    place = jnp.where((place_rows == group * nmode + mode) & (mode < nmode), 1.0, 0.0).astype(F32)
-    for k in range(columns // chunk):
-        high, low = split(jnp.dot(
-            cfull[:, k * chunk:(k + 1) * chunk], place, precision=highest, preferred_element_type=F32))
-        cpad[0:5 * unit, k * padded:(k + 1) * padded] = high
-        cpad[5 * unit:10 * unit, k * padded:(k + 1) * padded] = low
-
     def coarse(terms):
         high, low = split(terms)
         both = jnp.dot(cpad[...], jnp.concatenate([high, low], axis=1), preferred_element_type=F32)
@@ -360,6 +345,20 @@
 
     lax.fori_loop(0, 4, first_outer, 0)
     lax.fori_loop(4, 8, first_inner, 0)
+    columns = call.shape[-1]
+    chunk = nmode * LANES // 2
+    if columns % chunk:
+        chunk = columns
+    padded = chunk // nmode * PAD
+    place_rows = lax.broadcasted_iota(jnp.int32, (chunk, padded), 0)
+    place_cols = lax.broadcasted_iota(jnp.int32, (chunk, padded), 1)
+    group, mode = place_cols >> 3, place_cols & (PAD - 1)
+    place = jnp.where((place_rows == group * nmode + mode) & (mode < nmode), 1.0, 0.0).astype(F32)
+    for k in range(columns // chunk):
+        high, low = split(jnp.dot(
+            cfull[:, k * chunk:(k + 1) * chunk], place, precision=highest, preferred_element_type=F32))
+        cpad[0:5 * unit, k * padded:(k + 1) * padded] = high
+        cpad[5 * unit:10 * unit, k * padded:(k + 1) * padded] = low
     _, coeff = gather(0, fold(image_terms(0)))
     wait_halo_sent(0)
     side = spread_side(coeff)
@@ -414,8 +413,15 @@
         if last:
             for b in range(nblk):
                 s = inv_ref[b]
-                out_ref[0, b] = mult[s] + length * dire[s]
-                out_ref[1, b] = proj[s]
+                res[b] = mult[s] + length * dire[s]
+            mult_copy = pltpu.make_async_copy(res, out_ref.at[0], loads_sem)
+            mult_copy.start()
+            for b in range(nblk):
+                ybuf[b] = proj[inv_ref[b]]
+            proj_copy = pltpu.make_async_copy(ybuf, out_ref.at[1], ops_sem.at[0])
+            proj_copy.start()
+            mult_copy.wait()
+            proj_copy.wait()
         else:
             def step_multipliers():
                 for g in range(8):
@@ -453,7 +459,7 @@
             functools.partial(kernel, nc, ns, parts, face),
             out_shape=out,
             in_specs=[smem, smem, anym, anym, vmem, vmem, vmem],
-            out_specs=vmem,
+            out_specs=anym,
             scratch_shapes=[
                 pltpu.VMEM((nblk, blk, order), BF16),
                 vec, vec, vec, vec, vec,

time: 114 us -> 114 us (level)
  no operation moved by 1% of the time
where the time goes in v4:
time: 114 us
  Pallas kernels  107 us (94%)
  local copies, waits for them, and re-layouts  4.73 us (4%)
  other arithmetic  1.25 us (1%)
    pallas_call x1, Pallas kernels, on_device(): pl.pallas_call(functools.partial(kernel, nc, ns, parts, face), out_shape=...  107 us
    slice x1, local copies, waits for them, and re-layouts, on_device(): both[1].reshape(local_loads.shape)  4.73 us

profile of v4, /device:TPU:0, one launch (start us, length us, event | category | flops | bytes accessed | tf_op | source)
XLA Modules:
  0.0 113.8 jit_solution(3965063682761435210)
XLA Ops:
  0.6 1.3 %select_reduce_fusion.inv_ref = s32[32]{0:T(128)} fusion(s32[32]{0:T(128)} %bitcast.11), kind=kLoop, calls=%fused_computation | loop fusion | flops 3040 | bytes 256 | tf_op jit(solution)/shard_map/reduce_sum | solution.py:450
  1.9 107.2 %shard_map.77 = f32[2,32,128,128]{3,2,1,0:T(8,128)} custom-call(s32[1,32]{1,0:T(1,128)} %slot_ref.1, s32[32]{0:T(128)} %select_reduce_fusion.inv_ref, bf16[32,128,2048]{2,1,0:T(8,128)(2,1)} %bitcast.8, f32[32,128,128]{2,1,0:T(8,128)} %bitcast.9, f32[6,2,2048]{2,1,0:T(2,128)} %bitcast.10, f32[12,384]{1,0:T(8,128)} %cmat_ref.1, f32[384,128]{1,0:T(8,128)} %cload_ref.1), custom_call_target="tpu_custom_call" | custom-call | flops 8589934592 | bytes 25165824 | tf_op jit(solution)/shard_map/pallas_call | solution.py:458
  109.1 4.7 %fusion = (f32[1,32,128,128]{3,2,1,0:T(8,128)}, f32[1,32,128,128]{3,2,1,0:T(8,128)}) fusion(f32[2,32,128,128]{3,2,1,0:T(8,128)} %shard_map.77), kind=kLoop, calls=%fused_computation.2 | loop fusion | bytes 8388608 | tf_op jit(solution)/shard_map/slice | solution.py:488
